TPU v7x, 128 devices: a whole 4x4x4 slice. The times are simulated.
128 devices in a mesh: seq: 32 (over z, x, core), exp: 4 (over y).
Axes of the slice: x: 4, y: 4, z: 4, core: 2. Of those that a mesh axis runs over, the one named last changes fastest.
Arguments:
- text_rows: bfloat16 [4096, 4096], P('seq', 'exp'), may hold values from -6 to 6
- image_rows: bfloat16 [2048, 4096], P('seq', 'exp'), may hold values from -6 to 6
- image_dest: int32 [2048], P('seq'), may hold values from 0 to 4095, as said below
- norm_gain: float32 [4096], replicated, may hold values from 0.5 to 1.5
- expert_ids: int32 [4096, 8], P('seq'), may hold values from 0 to 63, all different within a row; in each aligned block of 128 rows (0 to 127, 128 to 255, ...) at most 32 rows name the same one
- gate_weights: float32 [4096, 8], P('seq'), may hold values from 0.1 to 1
- w_gate: bfloat16 [64, 4096, 1536], P('seq', None, 'exp'), may hold values from -0.09375 to 0.09375
- w_up: bfloat16 [64, 4096, 1536], P('seq', None, 'exp'), may hold values from -0.09375 to 0.09375
- w_down: bfloat16 [64, 1536, 4096], P('seq', 'exp'), may hold values from -0.15625 to 0.15625
Outputs:
- block_out: bfloat16 [4096, 4096], P('seq', 'exp')
Inputs may be any that keep to these rules, and one draw needn't show every extreme that they name: `image_dest`: all positions are distinct. The 64 rows of one index of seq go to consecutive positions (modulo 4096) that meet at most two blocks of 128 tokens; in every draw some block receives all 64 rows of one index. `expert_ids`: each row names 8 different experts; in each aligned block of 128 rows (the tokens of one index of seq) no expert is named by more than 32 rows, and in some block one expert is named by exactly 32.
All inputs are finite; a program needn't handle non-finite values.
Results may differ from a plain program's by a relative error of at most 0.015.
Values may be sent and summed in bfloat16 or wider, within the bound.
A program may use at most 192 MiB of HBM per device.

v0:
```python
import jax
import jax.numpy as jnp
from jax import lax
from jax.sharding import PartitionSpec as P


def on_device(
    text_rows, image_rows, image_dest, norm_gain, expert_ids, gate_weights, w_gate, w_up, w_down
):
    seq_count = lax.axis_size("seq")
    tok_dev = text_rows.shape[0]
    quarter = text_rows.shape[1]
    img_dev = image_rows.shape[0]
    exp_dev = w_gate.shape[0]
    top = expert_ids.shape[1]
    experts = exp_dev * seq_count
    capacity = 2 * tok_dev * top // experts
    width = quarter * lax.axis_size("exp")
    owner = image_dest // tok_dev
    owner_hot = (owner[:, None] == jnp.arange(seq_count, dtype=jnp.int32)[None, :]).astype(
        jnp.int32
    )
    within = jnp.sum(jnp.cumsum(owner_hot, axis=0) * owner_hot, axis=1) - 1
    image_slot = owner * img_dev + within
    send_rows = (
        jnp.zeros((seq_count * img_dev, quarter), jnp.bfloat16).at[image_slot].set(image_rows)
    )
    send_where = (
        jnp.full((seq_count * img_dev,), -1, jnp.int32).at[image_slot].set(image_dest % tok_dev)
    )
    got_rows, got_where = (
        lax.all_to_all(
            send_rows.reshape(seq_count, img_dev, quarter),
            "seq",
            split_axis=0,
            concat_axis=0,
            tiled=True,
        ),
        lax.all_to_all(
            send_where.reshape(seq_count, img_dev), "seq", split_axis=0, concat_axis=0, tiled=True
        ),
    )
    place_hot = jnp.arange(tok_dev, dtype=jnp.int32)[:, None] == got_where.reshape(1, -1)
    placed = jnp.dot(
        place_hot.astype(jnp.bfloat16),
        got_rows.reshape(-1, quarter),
        preferred_element_type=jnp.float32,
    )
    present = jnp.any(place_hot, axis=1)
    merged = jnp.where(present[:, None], placed.astype(jnp.bfloat16), text_rows)
    merged_f = merged.astype(jnp.float32)
    flat_ids = expert_ids.reshape(-1)
    expert_hot = (flat_ids[:, None] == jnp.arange(experts, dtype=jnp.int32)[None, :]).astype(
        jnp.int32
    )
    rank = jnp.sum(jnp.cumsum(expert_hot, axis=0) * expert_hot, axis=1) - 1
    slots = flat_ids * capacity + rank
    source_tok = jnp.arange(tok_dev * top, dtype=jnp.int32) // top
    whole = lax.all_gather(merged, "exp", axis=1, tiled=True).astype(jnp.float32)
    scale = lax.rsqrt(jnp.mean(whole * whole, axis=1, keepdims=True) + 1e-06)
    normed = (whole * scale * norm_gain).astype(jnp.bfloat16)
    outgoing = (
        jnp.zeros((experts * capacity, width), jnp.bfloat16).at[slots].set(normed[source_tok])
    )
    arrived = lax.all_to_all(
        outgoing.reshape(seq_count, exp_dev * capacity, width),
        "seq",
        split_axis=0,
        concat_axis=0,
        tiled=True,
    )
    grouped = arrived.reshape(seq_count, exp_dev, capacity, width)
    gate_part = jnp.einsum("secd,edf->secf", grouped, w_gate, preferred_element_type=jnp.float32)
    up_part = jnp.einsum("secd,edf->secf", grouped, w_up, preferred_element_type=jnp.float32)
    hidden = (jax.nn.silu(gate_part) * up_part).astype(jnp.bfloat16)
    partial_out = jnp.einsum("secf,efd->secd", hidden, w_down, preferred_element_type=jnp.float32)
    summed = lax.psum_scatter(
        partial_out.astype(jnp.bfloat16), "exp", scatter_dimension=3, tiled=True
    )
    returned = lax.all_to_all(
        summed.reshape(seq_count, exp_dev * capacity, quarter),
        "seq",
        split_axis=0,
        concat_axis=0,
        tiled=True,
    )
    picked = returned.reshape(experts * capacity, quarter)[slots].astype(jnp.float32)
    picked = picked.reshape(tok_dev, top, quarter)
    mixture = jnp.einsum("tk,tkd->td", gate_weights, picked)
    return (merged_f + mixture).astype(jnp.bfloat16)


def solution(mesh):
    placed = (
        P("seq", "exp"),
        P("seq", "exp"),
        P("seq"),
        P(),
        P("seq", None),
        P("seq", None),
        P("seq", None, "exp"),
        P("seq", None, "exp"),
        P("seq", "exp", None),
    )
    return jax.shard_map(
        on_device, mesh=mesh, in_specs=placed, out_specs=P("seq", "exp"), check_vma=False
    )
```

profile of v0, /device:TPU:0, one launch (start us, length us, event | category | flops | bytes accessed | tf_op | source)
XLA Modules:
  0.0 608.1 jit_solution(7892075014201817361)
XLA Ops:
  7.6 0.8 scatter_custom_fusion
  9.1 8.2 %all-to-all-start = ((s32[32,1,64]{2,1,0:T(1,128)}), s32[32,1,64]{2,1,0:T(1,128)S(1)}, u32[]{:S(2)}, u32[]{:S(2)}) async-start(s32[32,1,64]{2,1,0:T(1,128)} %all_to_all.15), calls=%async_computation | async-start | bytes 32768 | tf_op jit(solution)/shard_map/all_to_all | solution.py:39
  17.3 4.1 scatter_custom_fusion.1
  21.4 3.2 all-to-all-done
  24.6 5.0 all-to-all-start.1
  31.4 51.6 %all-to-all-done.1 = bf16[32,64,1024]{2,1,0:T(8,128)(2,1)} async-done(((bf16[32,64,1024]{2,1,0:T(8,128)(2,1)}), bf16[32,64,1024]{2,1,0:T(8,128)(2,1)}, u32[]{:S(2)}, u32[]{:S(2)}) %all-to-all-start.1) | async-done | bytes 4194336 | tf_op jit(solution)/shard_map/all_to_all | solution.py:32
  83.1 3.6 fusion.29
  87.0 18.0 %reduce-window.6 = s32[64,8,128]{2,1,0:T(8,128)S(1)} reduce-window(s32[64,8,128]{2,1,0:T(8,128)S(1)} %fusion.35, s32[]{:T(128)} %constant.67.clone.1), window={size=1x1x128 pad=0_0x0_0x127_0}, to_apply=%region_5.6 | reduce-window | flops 8323072 | bytes 524292 | tf_op jit(solution)/shard_map/reduce-window
  105.9 2.0 all-gather.2.cloned.1.call-done
  107.9 1.5 fusion.13
  109.4 1.5 fusion.15
  111.0 7.7 %gather_fusion = bf16[1024,4096]{1,0:T(8,128)(2,1)} fusion(bf16[128,4096]{1,0:T(8,128)(2,1)S(1)} %fusion.15, s32[1024]{0:T(1024)S(1)} %broadcast_clamp_fusion.1), kind=kCustom, calls=%fused_computation | custom fusion | bytes 16781312 | tf_op jit(solution)/shard_map/gather | solution.py:63
  118.7 22.0 %scatter_custom_fusion.2 = bf16[2048,4096]{1,0:T(8,128)(2,1)} fusion(s32[1024]{0:T(1024)S(1)} %bitcast.82, bf16[1024,4096]{1,0:T(8,128)(2,1)} %gather_fusion, bf16[]{:T(256)} %constant.74.clone.1), kind=kCustom, calls=%fused_computation.10 | custom fusion | bytes 16777728 | tf_op jit(solution)/shard_map/scatter | solution.py:63
  140.7 193.2 %all_to_all.24 = bf16[32,64,4096]{2,1,0:T(8,128)(2,1)S(1)} all-to-all(bf16[32,64,4096]{2,1,0:T(8,128)(2,1)} %bitcast.75), channel_id=1, replica_groups=mesh['seq'=32,'exp'=4] {'seq'}, dimensions={0} | all-to-all | bytes 33554432 | tf_op jit(solution)/shard_map/all_to_all | solution.py:65
  333.9 5.7 copy-done
  339.6 12.0 %fusion.2 = f32[2,32,32,384]{3,2,1,0:T(8,128)} fusion(bf16[32,2,32,4096]{3,2,1,0:T(8,128)(2,1)S(1)} %bitcast.76, bf16[2,4096,384]{2,1,0:T(8,128)(2,1)} %param.15), kind=kOutput, calls=%fused_computation.8 | convolution fusion | flops 6442450944 | bytes 26214400 | tf_op jit(solution)/shard_map/secd,edf->secf/dot_general | solution.py:73
  351.6 26.2 %convert_bitcast_fusion = bf16[32,2,32,4096]{3,2,0,1:T(8,128)(2,1)} fusion(bf16[2,384,4096]{2,1,0:T(8,128)(2,1)} %param.17, f32[2,32,32,384]{3,2,1,0:T(8,128)} %fusion.2, bf16[2,4096,384]{2,1,0:T(8,128)(2,1)} %param.16, bf16[32,2,32,4096]{3,2,1,0:T(8,128)(2,1)} %bitcast.77), kind=kOutput, calls=%fused_computation.5 | convolution fusion | flops 12898009088 | bytes 49283072 | tf_op jit(solution)/shard_map/secf,efd->secd/dot_general | solution.py:76
  377.9 148.2 %reduce-scatter.2.cloned.1.call-done = bf16[32,2,32,1024]{3,2,0,1:T(8,128)(2,1)} async-done(((bf16[32,2,32,4096]{3,2,0,1:T(8,128)(2,1)}), bf16[32,2,32,1024]{3,2,0,1:T(8,128)(2,1)}) %reduce-scatter.2.cloned.1.call-update) | async-done | bytes 4194320 | tf_op jit(solution)/shard_map/reduce_scatter | solution.py:77
  526.1 4.9 copy.24
  531.0 7.5 %all-to-all-start.3 = ((bf16[32,64,1024]{2,1,0:T(8,128)(2,1)}), bf16[32,64,1024]{2,1,0:T(8,128)(2,1)}, u32[]{:S(2)}, u32[]{:S(2)}) async-start(bf16[32,64,1024]{2,1,0:T(8,128)(2,1)} %bitcast.79), calls=%async_computation.4 | async-start | bytes 8388608 | tf_op jit(solution)/shard_map/all_to_all | solution.py:80
  538.7 53.3 %all-to-all-done.3 = bf16[32,64,1024]{2,1,0:T(8,128)(2,1)} async-done(((bf16[32,64,1024]{2,1,0:T(8,128)(2,1)}), bf16[32,64,1024]{2,1,0:T(8,128)(2,1)}, u32[]{:S(2)}, u32[]{:S(2)}) %all-to-all-start.3) | async-done | bytes 4194336 | tf_op jit(solution)/shard_map/all_to_all | solution.py:80
  592.0 7.7 %gather_fusion.1 = bf16[1024,1024]{1,0:T(8,128)(2,1)S(1)} fusion(bf16[2048,1024]{1,0:T(8,128)(2,1)} %bitcast.19, s32[1024]{0:T(1024)S(1)} %broadcast_clamp_fusion), kind=kCustom, calls=%fused_computation.1 | custom fusion | bytes 4198400 | tf_op jit(solution)/shard_map/gather | solution.py:87
  599.8 0.7 fusion.16
  600.5 0.8 fusion.31
  (46 shorter events, 4.8 us)
Async XLA Ops:
  9.1 15.5 %all-to-all-start = ((s32[32,1,64]{2,1,0:T(1,128)}), s32[32,1,64]{2,1,0:T(1,128)S(1)}, u32[]{:S(2)}, u32[]{:S(2)}) async-start(s32[32,1,64]{2,1,0:T(1,128)} %all_to_all.15), calls=%async_computation | async-start | bytes 32768 | tf_op jit(solution)/shard_map/all_to_all | solution.py:39
  24.6 5.0 copy-start.4
  24.6 58.5 %copy-start.2 = (bf16[128,1024]{1,0:T(8,128)(2,1)S(1)}, bf16[128,1024]{1,0:T(8,128)(2,1)}, u32[]{:S(2)}) copy-start(bf16[128,1024]{1,0:T(8,128)(2,1)} %param.9) | copy-start | bytes 786436
  24.6 58.5 %all-to-all-start.1 = ((bf16[32,64,1024]{2,1,0:T(8,128)(2,1)}), bf16[32,64,1024]{2,1,0:T(8,128)(2,1)}, u32[]{:S(2)}, u32[]{:S(2)}) async-start(bf16[32,64,1024]{2,1,0:T(8,128)(2,1)} %bitcast.78), calls=%async_computation.1 | async-start | bytes 8388608 | tf_op jit(solution)/shard_map/all_to_all | solution.py:32
  29.6 78.3 %all-gather.2.cloned.1.call-start = ((), (), s32[]{:S(2)}) async-start(), calls=%async_computation.5 | async-start | bytes 1310720 | tf_op jit(solution)/shard_map/all_gather | solution.py:59
  83.1 26.4 %copy-start.3 = (f32[4096]{0:T(1024)S(1)}, f32[4096]{0:T(1024)}, u32[]{:S(2)}) copy-start(f32[4096]{0:T(1024)} %param.12) | copy-start | bytes 49156
  86.7 439.4 %reduce-scatter.2.cloned.1.call-start = ((), (), s32[]{:S(2)}) async-start(), calls=%async_computation.6 | async-start | bytes 20971520 | tf_op jit(solution)/shard_map/reduce_scatter | solution.py:77
  333.9 5.7 copy-start
  531.0 7.5 %copy-start.5 = (f32[128,8]{0,1:T(8,128)S(1)}, f32[128,8]{0,1:T(8,128)}, u32[]{:S(2)}) copy-start(f32[128,8]{0,1:T(8,128)} %param.14) | copy-start | bytes 12292
  531.0 61.0 %all-to-all-start.3 = ((bf16[32,64,1024]{2,1,0:T(8,128)(2,1)}), bf16[32,64,1024]{2,1,0:T(8,128)(2,1)}, u32[]{:S(2)}, u32[]{:S(2)}) async-start(bf16[32,64,1024]{2,1,0:T(8,128)(2,1)} %bitcast.79), calls=%async_computation.4 | async-start | bytes 8388608 | tf_op jit(solution)/shard_map/all_to_all | solution.py:80
  592.0 8.5 %copy-start.1 = (bf16[128,1024]{1,0:T(8,128)(2,1)S(1)}, bf16[128,1024]{1,0:T(8,128)(2,1)}, u32[]{:S(2)}) copy-start(bf16[128,1024]{1,0:T(8,128)(2,1)} %fusion.29) | copy-start | bytes 786436
Sparse Core Ops, SparseCore 0:
  86.8 21.0 all-gather.1
  378.0 148.0 reduce-scatter.1
where the time goes:
time: 609 us; the launch traced here: 608 us
  waiting for transfers between devices  258 us (42%)
  blocking collectives  193 us (32%)
  local copies, waits for them, and re-layouts  55.2 us (9%)
  matrix products  42.5 us (7%)
  other arithmetic  24.1 us (4%)
  starting transfers between devices  21 us (3%)
  between operations  13.6 us (2%)
    all_to_all x1, blocking collectives, on_device(): lax.all_to_all(outgoing.reshape(seq_count, exp_dev * capacity, width), 's...  193 us
    reduce_scatter x1, waiting for transfers between devices, on_device(): lax.psum_scatter(partial_out.astype(jnp.bfloat16), 'exp', scatter_dimensi...  148 us
    all_to_all x1, waiting for transfers between devices, on_device(): lax.all_to_all(summed.reshape(seq_count, exp_dev * capacity, quarter), 's...  53.3 us
    all_to_all x1, waiting for transfers between devices, on_device(): lax.all_to_all(send_rows.reshape(seq_count, img_dev, quarter), 'seq', spl...  51.6 us
    dot_general x1, matrix products, on_device(): jnp.einsum('secf,efd->secd', hidden, w_down, preferred_element_type=jnp.f...  26.2 us
    scatter x1, local copies, waits for them, and re-layouts, on_device(): jnp.zeros((experts * capacity, width), jnp.bfloat16).at[slots]  22 us
    another operation x3, other arithmetic  18.2 us
  transfers between devices with their start and end apart: 5, of which 5 were waited for; matrix products, arithmetic and copies ran while one was open for 4% of the time, Pallas kernels for 0%

commit v1 on v0

v1 whole, which is shorter than its diff:
```python
import functools

import jax
import jax.numpy as jnp
from jax import lax
from jax.experimental import pallas as pl
from jax.experimental.pallas import tpu as pltpu
from jax.sharding import PartitionSpec as P

MESH = pl.DeviceIdType.MESH
CHUNKS = 4
ROWS = 32
QUARTER = 1024
DIMS = "yzx"
ORDERS = ("xyz", "yzx", "zxy")
WIDTHS = ((384, 384, 256), (384, 256, 384), (256, 384, 384), (384, 384, 256))
UNITS = 4
TILES = 8
TILE = 512


def place():
    s = lax.axis_index("seq")
    return {"z": s // 8, "x": (s // 2) % 4, "y": lax.axis_index("exp")}, s % 2


def device(at, core):
    return ((at["z"] * 4 + at["x"]) * 2 + core, at["y"])


def moved(at, axis, by):
    new = dict(at)
    new[axis] = (at[axis] + by + 4) % 4
    return new


def columns(q, p):
    return pl.ds(sum(WIDTHS[q][:p]), WIDTHS[q][p])


def expert_kernel(
    normed, merged, gates, w_gate, w_up, w_down,
    out, far_gate, far_up, far_down,
    X, H, WB, WD, half1, half2, half3, full1, full2, full3,
    own_sem, wb_sem, wd_sem, far_send, far_recv, ag_send, ag_recv, rs_send, rs_recv,
):
    me, core = place()
    barrier = pltpu.get_barrier_semaphore()
    neighbours = [device(moved(me, a, d), core) for a in "xyz" for d in (1, -1)]
    neighbours.append(device(me, 1 - core))
    for who in neighbours:
        pl.semaphore_signal(barrier, inc=1, device_id=who, device_id_type=MESH)
    pl.semaphore_wait(barrier, len(neighbours))

    def slab(q, full, at, cols, rows=pl.ds(0, ROWS)):
        index = tuple(slice(None) if a in full else at[a] for a in DIMS)
        return (q, *index, rows, cols)

    far = [
        pltpu.make_async_remote_copy(
            src_ref=src, dst_ref=dst, send_sem=far_send.at[i], recv_sem=far_recv.at[i],
            device_id=device(me, 1 - core), device_id_type=MESH,
        )
        for i, (src, dst) in enumerate(
            ((w_gate, far_gate), (w_up, far_up), (w_down, far_down))
        )
    ]
    own = [
        pltpu.make_async_copy(
            normed.at[pl.ds(ROWS * q, ROWS)], X.at[q, me["y"], me["z"], me["x"]], own_sem.at[q]
        )
        for q in range(CHUNKS)
    ]

    def ag_copy(q, p, k, j):
        order = ORDERS[p]
        axis, full = order[k], order[:k]
        way = 1 if j % 2 == 0 else -1
        cols = columns(q, p)
        if j < 2:
            index = slab(q, full, me, cols)
            src = normed.at[pl.ds(ROWS * q, ROWS), cols] if k == 0 else X.at[index]
        else:
            rows = pl.ds(0, 16) if j == 2 else pl.ds(16, 16)
            index = slab(q, full, moved(me, axis, -way), cols, rows)
            src = X.at[index]
        return pltpu.make_async_remote_copy(
            src_ref=src, dst_ref=X.at[index],
            send_sem=ag_send.at[q, p, k, j], recv_sem=ag_recv.at[q, p, k, j],
            device_id=device(moved(me, axis, way), core), device_id_type=MESH,
        )

    def ag_first(q, k):
        for p in range(3):
            if k:
                for j in (2, 3):
                    ag_copy(q, p, k - 1, j).wait_recv()
            for j in (0, 1):
                ag_copy(q, p, k, j).start()

    def ag_second(q, k):
        for p in range(3):
            for j in (0, 1):
                ag_copy(q, p, k, j).wait_recv()
                ag_copy(q, p, k, j + 2).start()

    def ag_end(q):
        for p in range(3):
            for j in (2, 3):
                ag_copy(q, p, 2, j).wait_recv()
            for k in range(3):
                for j in range(4):
                    ag_copy(q, p, k, j).wait_send()

    halves, fulls = (half1, half2, half3), (full1, full2, full3)

    def rs_refs(q, p, k, j):
        order = ORDERS[p][::-1]
        axis, full = order[k], order[k + 1:]
        cols = columns(q, p)
        way = 1 if j % 2 == 0 else -1
        mid = (slice(None),) * len(full)
        if j < 2:
            rows = pl.ds(0, 16) if j == 0 else pl.ds(16, 16)
            sent = slab(q, full, moved(me, axis, 2), cols, rows)
            kept = slab(q, full, moved(me, axis, way), cols, rows)
            got = halves[k].at[(q, j, *mid, slice(None), cols)]
        else:
            sent = slab(q, full, moved(me, axis, way), cols)
            kept = slab(q, full, me, cols)
            got = fulls[k].at[(q, j - 2, *mid, slice(None), cols)]
        return sent, kept, got, device(moved(me, axis, way), core)

    def rs_copy(q, p, k, j):
        sent, _, got, who = rs_refs(q, p, k, j)
        return pltpu.make_async_remote_copy(
            src_ref=X.at[sent], dst_ref=got,
            send_sem=rs_send.at[q, p, k, j], recv_sem=rs_recv.at[q, p, k, j],
            device_id=who, device_id_type=MESH,
        )

    def rs_first(q, k):
        for p in range(3):
            for j in (0, 1):
                rs_copy(q, p, k, j).start()

    def f32(v):
        return v.astype(jnp.float32)

    def rs_second(q, k):
        for p in range(3):
            for j in (0, 1):
                rs_copy(q, p, k, j).wait_recv()
                _, kept, got, _ = rs_refs(q, p, k, j)
                X[kept] = (f32(X[kept]) + f32(got[...])).astype(jnp.bfloat16)
                rs_copy(q, p, k, j + 2).start()

    def rs_end(q, k):
        for p in range(3):
            _, kept, a, _ = rs_refs(q, p, k, 2)
            b = rs_refs(q, p, k, 3)[2]
            for j in (2, 3):
                rs_copy(q, p, k, j).wait_recv()
            total = f32(X[kept]) + f32(a[...]) + f32(b[...])
            if k < 2:
                X[kept] = total.astype(jnp.bfloat16)
                for j in (0, 1):
                    rs_copy(q, p, k + 1, j).start()
            else:
                rows, cols = pl.ds(ROWS * q, ROWS), columns(q, p)
                out[rows, cols] = (total + f32(merged[rows, cols])).astype(jnp.bfloat16)

    def wb_copies(slot, gate, up, e):
        return [
            pltpu.make_async_copy(gate.at[e], WB.at[slot, :, pl.ds(0, 384)], wb_sem.at[slot, 0]),
            pltpu.make_async_copy(up.at[e], WB.at[slot, :, pl.ds(384, 384)], wb_sem.at[slot, 1]),
        ]

    def wb_start(e, slot):
        @pl.when(e < 2)
        def _():
            for c in wb_copies(slot, w_gate, w_up, e):
                c.start()

        @pl.when(e >= 2)
        def _():
            for c in wb_copies(slot, far_gate, far_up, e - 2):
                c.start()

    def wd_copies(n, slot):
        cols = pl.ds(pl.multiple_of(n * TILE, TILE), TILE)
        return [
            pltpu.make_async_copy(w_down.at[:, :, cols], WD.at[slot, pl.ds(0, 2)], wd_sem.at[slot, 0]),
            pltpu.make_async_copy(far_down.at[:, :, cols], WD.at[slot, pl.ds(2, 2)], wd_sem.at[slot, 1]),
        ]

    plan = {
        (0, 0): [lambda: ag_second(1, 2), lambda: ag_first(2, 2)],
        (0, 3): [lambda: ag_second(2, 2), lambda: ag_first(3, 2)],
        (0, 8): [lambda: ag_second(3, 2)],
        (0, 11): [lambda: ag_end(1)],
        (1, 11): [lambda: ag_end(2)],
        (2, 11): [lambda: ag_end(3)],
    }

    def add(q, u, f, *args):
        plan.setdefault((q, u), []).append(lambda: f(*args))

    for q in range(CHUNKS):
        add(q, 11, rs_first, q, 0)
        if q < CHUNKS - 1:
            add(q + 1, 1, rs_second, q, 0)
            add(q + 1, 3, rs_end, q, 0)
            add(q + 1, 5, rs_second, q, 1)
            add(q + 1, 7, rs_end, q, 1)
            add(q + 1, 9, rs_second, q, 2)
            add(q + 1, 10, rs_end, q, 2)

    def hooks(q, u, units):
        for (pq, pu), actions in sorted(plan.items()):
            if pu in units:
                @pl.when((q == pq) & (u == pu))
                def _(actions=actions):
                    for act in actions:
                        act()

    for c in own:
        c.start()
    for q in range(CHUNKS):
        ag_first(q, 0)
    for c in far:
        c.start()
    wb_start(0, 0)
    for c in own:
        c.wait()
    for k in range(2):
        for q in range(CHUNKS):
            ag_second(q, k)
        for q in range(CHUNKS if k == 0 else 2):
            ag_first(q, k + 1)
    ag_second(0, 2)
    ag_end(0)

    def chunk(q, carry):
        def unit(e, carry):
            slot = lax.rem(e, 2)

            @pl.when((q == 0) & (e == 1))
            def _():
                for c in far:
                    c.wait_recv()

            @pl.when((e < UNITS - 1) | (q < CHUNKS - 1))
            def _():
                wb_start(lax.rem(e + 1, UNITS), 1 - slot)

            @pl.when(e == UNITS - 1)
            def _():
                for c in wd_copies(0, 0):
                    c.start()

            for c in wb_copies(slot, w_gate, w_up, 0):
                c.wait()

            def rows(m, carry):
                part = pl.ds(2 * m, 2)
                acc = jnp.zeros((256, 768), jnp.float32)
                for y in range(4):
                    acc += jnp.dot(
                        X[q, y, part].reshape(256, QUARTER),
                        WB[slot, pl.ds(QUARTER * y, QUARTER), :],
                        preferred_element_type=jnp.float32,
                    )
                g, u = acc[:, :384], acc[:, 384:]
                here = pl.ds(pl.multiple_of(256 * m, 256), 256)
                lane = lax.broadcasted_iota(jnp.int32, (256, 128), 1)
                weight = jnp.sum(jnp.where(lane == e, gates[q, here, :], 0.0), axis=1, keepdims=True)
                hidden = g / (1.0 + jnp.exp(-g)) * u * weight
                H[here, pl.ds(pl.multiple_of(e * 384, 128), 384)] = hidden.astype(jnp.bfloat16)
                return carry

            lax.fori_loop(0, 2, rows, 0)
            hooks(q, e, range(UNITS))
            return carry

        lax.fori_loop(0, UNITS, unit, 0)

        def tile(n, carry):
            slot = lax.rem(n, 2)

            @pl.when(n < TILES - 1)
            def _():
                for c in wd_copies(n + 1, 1 - slot):
                    c.start()

            for c in wd_copies(n, slot):
                c.wait()
            acc = jnp.dot(
                H[...], WD[slot].reshape(1536, TILE), preferred_element_type=jnp.float32
            )
            X[q, n // 2, :, :, :, pl.ds(pl.multiple_of(lax.rem(n, 2) * TILE, TILE), TILE)] = (
                acc.astype(jnp.bfloat16).reshape(4, 4, ROWS, TILE)
            )
            hooks(q, n + UNITS, range(UNITS, UNITS + TILES))
            return carry

        lax.fori_loop(0, TILES, tile, 0)
        return carry

    lax.fori_loop(0, CHUNKS, chunk, 0)
    last = CHUNKS - 1
    for k in range(3):
        rs_second(last, k)
        rs_end(last, k)
    for c in far:
        c.wait_send()
    for q in range(CHUNKS):
        for p in range(3):
            for k in range(3):
                for j in range(4):
                    rs_copy(q, p, k, j).wait_send()


def experts(normed, merged, gates, w_gate, w_up, w_down):
    bf = jnp.bfloat16
    hbm = pl.BlockSpec(memory_space=pl.ANY)
    vmem = pl.BlockSpec(memory_space=pltpu.VMEM)
    dma = pltpu.SemaphoreType.DMA
    flops = 2 * 2048 * 1536 * 4096 * 3
    return pl.pallas_call(
        expert_kernel,
        out_shape=[
            jax.ShapeDtypeStruct(merged.shape, bf),
            jax.ShapeDtypeStruct(w_gate.shape, bf),
            jax.ShapeDtypeStruct(w_up.shape, bf),
            jax.ShapeDtypeStruct(w_down.shape, bf),
        ],
        in_specs=[vmem, vmem, vmem, hbm, hbm, hbm],
        out_specs=[vmem, hbm, hbm, hbm],
        scratch_shapes=[
            pltpu.VMEM((CHUNKS, 4, 4, 4, ROWS, QUARTER), bf),
            pltpu.VMEM((512, 1536), bf),
            pltpu.VMEM((2, 4096, 768), bf),
            pltpu.VMEM((2, 4, 384, TILE), bf),
            pltpu.VMEM((CHUNKS, 2, 4, 4, 16, QUARTER), bf),
            pltpu.VMEM((CHUNKS, 2, 4, 16, QUARTER), bf),
            pltpu.VMEM((CHUNKS, 2, 16, QUARTER), bf),
            pltpu.VMEM((CHUNKS, 2, 4, 4, ROWS, QUARTER), bf),
            pltpu.VMEM((CHUNKS, 2, 4, ROWS, QUARTER), bf),
            pltpu.VMEM((CHUNKS, 2, ROWS, QUARTER), bf),
            dma((CHUNKS,)),
            dma((2, 2)),
            dma((2, 2)),
            dma((3,)),
            dma((3,)),
            dma((CHUNKS, 3, 3, 4)),
            dma((CHUNKS, 3, 3, 4)),
            dma((CHUNKS, 3, 3, 4)),
            dma((CHUNKS, 3, 3, 4)),
        ],
        cost_estimate=pl.CostEstimate(
            flops=flops, bytes_accessed=150 << 20, transcendentals=2048 * 1536
        ),
        compiler_params=pltpu.CompilerParams(
            collective_id=0, has_side_effects=True, vmem_limit_bytes=60 << 20
        ),
    )(normed, merged, gates, w_gate, w_up, w_down)[0]


def on_device(
    text_rows, image_rows, image_dest, norm_gain, expert_ids, gate_weights, w_gate, w_up, w_down
):
    seq_count = lax.axis_size("seq")
    tok_dev = text_rows.shape[0]
    s = lax.axis_index("seq")
    y = lax.axis_index("exp")
    rows_all = lax.all_gather(image_rows, "seq").reshape(-1, QUARTER)
    dest_all = lax.all_gather(image_dest, "seq").reshape(1, -1)
    place_hot = (jnp.arange(tok_dev, dtype=jnp.int32) + s * tok_dev)[:, None] == dest_all
    placed = jnp.dot(place_hot.astype(jnp.bfloat16), rows_all, preferred_element_type=jnp.float32)
    present = jnp.any(place_hot, axis=1)
    merged = jnp.where(present[:, None], placed.astype(jnp.bfloat16), text_rows)
    merged_f = merged.astype(jnp.float32)
    squares = lax.psum(jnp.sum(merged_f * merged_f, axis=1, keepdims=True), "exp")
    scale = lax.rsqrt(squares / 4096 + 1e-06)
    gain = lax.dynamic_slice(norm_gain, (y * QUARTER,), (QUARTER,))
    normed = (merged_f * scale * gain).astype(jnp.bfloat16)
    ids = lax.all_gather(expert_ids, "seq").reshape(16, 2, tok_dev, 8)
    weights = lax.all_gather(gate_weights, "seq").reshape(16, 2, tok_dev, 8)
    core = s % 2
    ids = lax.dynamic_index_in_dim(ids, core, 1, keepdims=False)
    weights = lax.dynamic_index_in_dim(weights, core, 1, keepdims=False)
    lane = jnp.arange(128, dtype=jnp.int32)
    chip = s - core
    expert = jnp.where(lane < 4, 2 * chip + (lane + 2 * core) % 4, -1)
    gates = jnp.sum(
        jnp.where(ids[..., None] == expert, weights[..., None], 0.0), axis=2
    )
    gates = gates.reshape(16, CHUNKS, ROWS, 128).transpose(1, 0, 2, 3).reshape(CHUNKS, 512, 128)
    return experts(normed, merged, gates, w_gate, w_up, w_down)


def solution(mesh):
    placed = (
        P("seq", "exp"),
        P("seq", "exp"),
        P("seq"),
        P(),
        P("seq", None),
        P("seq", None),
        P("seq", None, "exp"),
        P("seq", None, "exp"),
        P("seq", "exp", None),
    )
    return jax.shard_map(
        on_device, mesh=mesh, in_specs=placed, out_specs=P("seq", "exp"), check_vma=False
    )
```

time: 609 us -> 314 us (0.52)
  waiting for transfers between devices: 258 us -> 0.73 us
  Pallas kernels: 0 us -> 208 us
  blocking collectives: 193 us -> 75.5 us
  local copies, waits for them, and re-layouts: 55.2 us -> 4.91 us
  matrix products: 42.5 us -> 3.05 us
  starting transfers between devices: 21 us -> 0.01 us
  other arithmetic: 24.1 us -> 6.84 us
    pallas_call x0 -> x1, Pallas kernels: none -> 208 us  [experts(): pl.pallas_call(expert_kernel, out_shape=[jax.ShapeDtypeStruct(merged.shap...]
    all_to_all x1 -> x0, blocking collectives: 193 us -> none  [on_device(): lax.all_to_all(outgoing.reshape(seq_count, exp_dev * capacity, width), 's...]
    reduce_scatter x1 -> x0, waiting for transfers between devices: 148 us -> none  [on_device(): lax.psum_scatter(partial_out.astype(jnp.bfloat16), 'exp', scatter_dimensi...]
    all_to_all x3 -> x0, waiting for transfers between devices: 108 us -> none  [the longest x1 53.3 us: on_device(): lax.all_to_all(summed.reshape(seq_count, exp_dev * capacity, quarter), 's...]
    all_gather x0 -> x2, blocking collectives: none -> 50 us  [the longest x1 26 us: on_device(): weights = lax.all_gather(gate_weights, 'seq').reshape(16, 2, tok_dev, 8)]
    dot_general x4 -> x1, matrix products: 42.5 us -> 3.05 us  [on_device(): jnp.dot(place_hot.astype(jnp.bfloat16), rows_all, preferred_element_type=...]
    scatter x3 -> x0, local copies, waits for them, and re-layouts: 26.8 us -> none  [the longest x1 22 us: on_device(): jnp.zeros((experts * capacity, width), jnp.bfloat16).at[slots]]
    all_to_all x3 -> x0, starting transfers between devices: 20.7 us -> none  [the longest x1 8.25 us: on_device(): lax.all_to_all(send_where.reshape(seq_count, img_dev), 'seq', split_axis=...]
  transfers between devices with their start and end apart: 5 -> 1, of which waited for: 5 -> 0; matrix products, arithmetic and copies ran while one was open for 4% -> 3% of each run, Pallas kernels for 0% -> 0%
where the time goes in v1:
time: 314 us; the launch traced here: 313 us
  Pallas kernels  208 us (66%)
  blocking collectives  75.5 us (24%)
  between operations  14.1 us (4%)
  other arithmetic  6.84 us (2%)
  local copies, waits for them, and re-layouts  4.91 us (2%)
    pallas_call x1, Pallas kernels, experts(): pl.pallas_call(expert_kernel, out_shape=[jax.ShapeDtypeStruct(merged.shap...  208 us
    all_gather x1, blocking collectives, on_device(): weights = lax.all_gather(gate_weights, 'seq').reshape(16, 2, tok_dev, 8)  26 us
    all_gather x1, blocking collectives, on_device(): ids = lax.all_gather(expert_ids, 'seq').reshape(16, 2, tok_dev, 8)  23.9 us
    unnamed x1, blocking collectives  14.6 us
    psum x1, blocking collectives, on_device(): lax.psum(jnp.sum(merged_f * merged_f, axis=1, keepdims=True), 'exp')  10.9 us
  transfers between devices with their start and end apart: 1, of which 0 were waited for; matrix products, arithmetic and copies ran while one was open for 3% of the time, Pallas kernels for 0%

profile of v1, /device:TPU:0, one launch (start us, length us, event | category | flops | bytes accessed | tf_op | source)
XLA Modules:
  0.0 312.8 jit_solution(8819541970518984899)
XLA Ops:
  6.5 0.0 copy-start.2
  6.5 0.0 all-gather.6.cloned.1.call-start
  6.5 0.7 all-gather.6.cloned.1.call-update
  7.3 26.0 %all-gather.3 = f32[4096,8]{0,1:T(8,128)S(1)} all-gather(f32[128,8]{0,1:T(8,128)} %param.14), channel_id=5, replica_groups=mesh['seq'=32,'exp'=4] {'seq'}, dimensions={0}, use_global_device_ids=true | all-gather | bytes 135168 | tf_op jit(solution)/shard_map/all_gather | solution.py:389
  33.3 0.3 copy.14
  33.6 23.9 %all-gather.2 = s32[4096,8]{0,1:T(8,128)S(1)} all-gather(s32[128,8]{0,1:T(8,128)} %param.13), channel_id=4, replica_groups=mesh['seq'=32,'exp'=4] {'seq'}, dimensions={0}, use_global_device_ids=true | all-gather | bytes 135168 | tf_op jit(solution)/shard_map/all_gather | solution.py:388
  57.6 0.3 copy.13
  58.0 5.7 %select_reduce_fusion = f32[16,128,128]{2,1,0:T(8,128)S(1)} fusion(f32[16,128,8]{2,1,0:T(8,128)S(1)} %copy.14, s32[128]{0:T(128)S(1)} %compare_select_fusion.2, s32[16,128,8]{2,1,0:T(8,128)S(1)} %copy.13), kind=kLoop, calls=%fused_computation | loop fusion | flops 6029312 | bytes 1180160 | tf_op jit(solution)/shard_map/reduce_sum | solution.py:396
  63.7 1.1 copy.15
  64.7 0.0 copy-done.3
  64.7 0.6 dynamic-slice
  66.0 0.7 dynamic_slice.11
  66.7 0.0 copy-done.2
  66.7 0.2 dynamic-update-slice
  66.9 14.6 %all-reduce = s32[2048]{0:T(1024)S(1)} all-reduce(s32[2048]{0:T(1024)S(1)} %dynamic-update-slice), channel_id=2, replica_groups=mesh['seq'=32,'exp'=4] {'seq'}, use_global_device_ids=true, to_apply=%add | all-reduce | flops 2048 | bytes 16384
  81.4 0.3 compare_reduce_fusion
  81.7 0.0 all-gather.6.cloned.1.call-done
  81.7 0.0 copy-done.1
  81.7 3.1 fusion.8
  84.8 10.9 %psum.7 = f32[128,1]{0,1:T(1,128)S(1)} all-reduce(f32[128,1]{0,1:T(1,128)S(1)} %bitcast.19), channel_id=1, replica_groups=mesh['seq'=32,'exp'=4] {'exp'}, use_global_device_ids=true, to_apply=%region_2.3 | all-reduce | flops 128 | bytes 1024 | tf_op jit(solution)/shard_map/psum | solution.py:384
  95.8 0.8 fusion.10.normed
  96.6 0.0 copy-done
  96.6 207.7 %shard_map.91 = (bf16[128,1024]{1,0:T(8,128)(2,1)}, bf16[2,4096,384]{2,1,0:T(8,128)(2,1)}, bf16[2,4096,384]{2,1,0:T(8,128)(2,1)}, bf16[2,384,4096]{2,1,0:T(8,128)(2,1)}) custom-call(bf16[128,1024]{1,0:T(8,128)(2,1)} %fusion.10.normed, bf16[128,1024]{1,0:T(8,128)(2,1)} %copy-done, f32[4,512,128]{2,1,0:T(8,128)} %bitcast.16, bf16[2,4096,384]{2,1,0:T(8,128)(2,1)} %w_gate.1, ...), custom_call_target="tpu_custom_call" | custom-call | flops 77309411328 | bytes 157286400 | tf_op jit(solution)/shard_map/pallas_call | solution.py:330
  304.3 1.7 copy.18
  (9 shorter events, 0.0 us)
Async XLA Ops:
  6.5 58.2 %copy-start.3 = (u32[128]{0:T(128)S(1)}, u32[128]{0:T(128)}, u32[]{:S(2)}) copy-start(u32[128]{0:T(128)} %constant.68) | copy-start | bytes 1540
  6.5 60.1 %copy-start.2 = (s32[64]{0:T(128)S(1)}, s32[64]{0:T(128)}, u32[]{:S(2)}) copy-start(s32[64]{0:T(128)} %param.11) | copy-start | bytes 772
  6.5 75.2 %copy-start.1 = (bf16[128,1024]{1,0:T(8,128)(2,1)S(1)}, bf16[128,1024]{1,0:T(8,128)(2,1)}, u32[]{:S(2)}) copy-start(bf16[128,1024]{1,0:T(8,128)(2,1)} %param.9) | copy-start | bytes 786436
  6.5 75.2 %all-gather.6.cloned.1.call-start = ((), (), s32[]{:S(2)}) async-start(), calls=%async_computation | async-start | bytes 4325376 | tf_op jit(solution)/shard_map/all_gather | solution.py:377
  84.8 11.8 %copy-start = (bf16[128,1024]{1,0:T(8,128)(2,1)}, bf16[128,1024]{1,0:T(8,128)(2,1)S(1)}, u32[]{:S(2)}) copy-start(bf16[128,1024]{1,0:T(8,128)(2,1)S(1)} %get-tuple-element.8.merged) | copy-start | bytes 786436
Sparse Core Ops, SparseCore 0:
  9.6 48.7 all-gather.5

commit v2 on v1

--- a/solution.py
+++ b/solution.py
@@ -62,7 +62,13 @@
             device_id=device(me, 1 - core), device_id_type=MESH,
         )
         for i, (src, dst) in enumerate(
-            ((w_gate, far_gate), (w_up, far_up), (w_down, far_down))
+            (
+                (w_gate.at[0], far_gate.at[0]),
+                (w_up.at[0], far_up.at[0]),
+                (w_gate.at[1], far_gate.at[1]),
+                (w_up.at[1], far_up.at[1]),
+                (w_down, far_down),
+            )
         )
     ]
     own = [
@@ -197,8 +203,8 @@
     plan = {
         (0, 0): [lambda: ag_second(1, 2), lambda: ag_first(2, 2)],
         (0, 3): [lambda: ag_second(2, 2), lambda: ag_first(3, 2)],
-        (0, 8): [lambda: ag_second(3, 2)],
         (0, 11): [lambda: ag_end(1)],
+        (1, 0): [lambda: ag_second(3, 2)],
         (1, 11): [lambda: ag_end(2)],
         (2, 11): [lambda: ag_end(3)],
     }
@@ -211,10 +217,11 @@
         if q < CHUNKS - 1:
             add(q + 1, 1, rs_second, q, 0)
             add(q + 1, 3, rs_end, q, 0)
-            add(q + 1, 5, rs_second, q, 1)
-            add(q + 1, 7, rs_end, q, 1)
-            add(q + 1, 9, rs_second, q, 2)
-            add(q + 1, 10, rs_end, q, 2)
+            add(q + 1, 6, rs_second, q, 1)
+            add(q + 1, 9, rs_end, q, 1)
+            add(q + 1, 11, rs_second, q, 2)
+            if q < CHUNKS - 2:
+                add(q + 2, 0, rs_end, q, 2)
 
     def hooks(q, u, units):
         for (pq, pu), actions in sorted(plan.items()):
@@ -228,27 +235,37 @@
         c.start()
     for q in range(CHUNKS):
         ag_first(q, 0)
-    for c in far:
+    for c in far[:2]:
         c.start()
     wb_start(0, 0)
     for c in own:
         c.wait()
-    for k in range(2):
-        for q in range(CHUNKS):
-            ag_second(q, k)
-        for q in range(CHUNKS if k == 0 else 2):
-            ag_first(q, k + 1)
+    ag_second(0, 0)
+    ag_first(0, 1)
+    for q in range(1, CHUNKS):
+        ag_second(q, 0)
+    for c in far[2:4]:
+        c.start()
+    ag_second(0, 1)
+    ag_first(0, 2)
+    for q in range(1, CHUNKS):
+        ag_first(q, 1)
+    far[4].start()
+    for q in range(1, CHUNKS):
+        ag_second(q, 1)
     ag_second(0, 2)
+    ag_first(1, 2)
     ag_end(0)
 
     def chunk(q, carry):
         def unit(e, carry):
             slot = lax.rem(e, 2)
 
-            @pl.when((q == 0) & (e == 1))
-            def _():
-                for c in far:
-                    c.wait_recv()
+            for first, ready in ((1, far[:2]), (2, far[2:4]), (3, far[4:])):
+                @pl.when((q == 0) & (e == first))
+                def _(ready=ready):
+                    for c in ready:
+                        c.wait_recv()
 
             @pl.when((e < UNITS - 1) | (q < CHUNKS - 1))
             def _():
@@ -262,24 +279,21 @@
             for c in wb_copies(slot, w_gate, w_up, 0):
                 c.wait()
 
-            def rows(m, carry):
-                part = pl.ds(2 * m, 2)
-                acc = jnp.zeros((256, 768), jnp.float32)
-                for y in range(4):
-                    acc += jnp.dot(
-                        X[q, y, part].reshape(256, QUARTER),
-                        WB[slot, pl.ds(QUARTER * y, QUARTER), :],
-                        preferred_element_type=jnp.float32,
-                    )
-                g, u = acc[:, :384], acc[:, 384:]
-                here = pl.ds(pl.multiple_of(256 * m, 256), 256)
-                lane = lax.broadcasted_iota(jnp.int32, (256, 128), 1)
-                weight = jnp.sum(jnp.where(lane == e, gates[q, here, :], 0.0), axis=1, keepdims=True)
-                hidden = g / (1.0 + jnp.exp(-g)) * u * weight
-                H[here, pl.ds(pl.multiple_of(e * 384, 128), 384)] = hidden.astype(jnp.bfloat16)
-                return carry
-
-            lax.fori_loop(0, 2, rows, 0)
+            acc = jnp.zeros((512, 768), jnp.float32)
+            for y in range(4):
+                acc += jnp.dot(
+                    X[q, y].reshape(512, QUARTER),
+                    WB[slot, pl.ds(QUARTER * y, QUARTER), :],
+                    preferred_element_type=jnp.float32,
+                )
+            g, u = acc[:, :384], acc[:, 384:]
+            lane = lax.broadcasted_iota(jnp.int32, (16, ROWS, 128), 2)
+            block = lax.broadcasted_iota(jnp.int32, (16, ROWS, 128), 0)
+            rows = gates[pl.ds(pl.multiple_of(q * ROWS, ROWS), ROWS), :]
+            weight = jnp.where(lane == 8 * block + e, rows[None], 0.0).reshape(512, 128)
+            weight = jnp.sum(weight, axis=1, keepdims=True)
+            hidden = g / (1.0 + jnp.exp(-g)) * u * weight
+            H[:, pl.ds(pl.multiple_of(e * 384, 128), 384)] = hidden.astype(jnp.bfloat16)
             hooks(q, e, range(UNITS))
             return carry
 
@@ -309,6 +323,7 @@
 
     lax.fori_loop(0, CHUNKS, chunk, 0)
     last = CHUNKS - 1
+    rs_end(last - 1, 2)
     for k in range(3):
         rs_second(last, k)
         rs_end(last, k)
@@ -351,8 +366,8 @@
             dma((CHUNKS,)),
             dma((2, 2)),
             dma((2, 2)),
-            dma((3,)),
-            dma((3,)),
+            dma((5,)),
+            dma((5,)),
             dma((CHUNKS, 3, 3, 4)),
             dma((CHUNKS, 3, 3, 4)),
             dma((CHUNKS, 3, 3, 4)),
@@ -367,36 +382,204 @@
     )(normed, merged, gates, w_gate, w_up, w_down)[0]
 
 
+IMAGES = ("zx", "xz")
+
+
+def image_kernel(
+    text, image, meta, gain,
+    merged, normed, gates,
+    IMG, META, SQ, GB,
+    im_send, im_recv, me_send, me_recv, sib_send, sib_recv, sq_send, sq_recv,
+):
+    me, core = place()
+    barrier = pltpu.get_barrier_semaphore()
+    neighbours = [device(moved(me, a, d), core) for a in "zx" for d in (1, -1)]
+    neighbours += [device(moved(me, "y", d), core) for d in (1, 2, 3)]
+    neighbours.append(device(me, 1 - core))
+    for who in neighbours:
+        pl.semaphore_signal(barrier, inc=1, device_id=who, device_id_type=MESH)
+    pl.semaphore_wait(barrier, len(neighbours))
+    z, x, y = me["z"], me["x"], me["y"]
+    IMG[core, z, x] = image[...]
+    META[core, z, x] = meta[...]
+
+    def spot(full, at):
+        return (core, *(slice(None) if a in full else at[a] for a in "zx"))
+
+    def im_copy(p, k, j):
+        axis, full = IMAGES[p][k], IMAGES[p][:k]
+        way = 1 if j % 2 == 0 else -1
+        at = me if j < 2 else moved(me, axis, -way)
+        rows = pl.ds(0, 64) if j < 2 else pl.ds(32 * (j - 2), 32)
+        part = IMG.at[(*spot(full, at), rows, pl.ds(512 * p, 512))]
+        return pltpu.make_async_remote_copy(
+            src_ref=part, dst_ref=part, send_sem=im_send.at[p, k, j], recv_sem=im_recv.at[p, k, j],
+            device_id=device(moved(me, axis, way), core), device_id_type=MESH,
+        )
+
+    def me_copy(k, j):
+        axis, full = IMAGES[0][k], IMAGES[0][:k]
+        way = 1 if j % 2 == 0 else -1
+        part = META.at[spot(full, me if j < 2 else moved(me, axis, -1))]
+        return pltpu.make_async_remote_copy(
+            src_ref=part, dst_ref=part, send_sem=me_send.at[k, j], recv_sem=me_recv.at[k, j],
+            device_id=device(moved(me, axis, way), core), device_id_type=MESH,
+        )
+
+    def sibling(part, i, j):
+        return pltpu.make_async_remote_copy(
+            src_ref=part, dst_ref=part, send_sem=sib_send.at[i, j], recv_sem=sib_recv.at[i, j],
+            device_id=device(me, 1 - core), device_id_type=MESH,
+        )
+
+    def sib_image(p, k, d):
+        full = IMAGES[p][:k]
+        at = moved(me, IMAGES[p][k], d)
+        part = IMG.at[(*spot(full, at), slice(None), pl.ds(512 * p, 512))]
+        return sibling(part, p, 3 * k + d)
+
+    shared = []
+    for p in range(2):
+        shared.append(sib_image(p, 0, 0))
+    for c in shared:
+        c.start()
+    for k in range(2):
+        for j in (0, 1):
+            me_copy(k, j).start()
+            for p in range(2):
+                im_copy(p, k, j).start()
+        me_copy(k, 0).wait_recv()
+        me_copy(k, 2).start()
+        for j in (0, 1):
+            for p in range(2):
+                im_copy(p, k, j).wait_recv()
+                im_copy(p, k, j + 2).start()
+                shared.append(sib_image(p, k, 3 if j == 0 else 1))
+                shared[-1].start()
+        me_copy(k, 1).wait_recv()
+        me_copy(k, 2).wait_recv()
+        for p in range(2):
+            for j in (2, 3):
+                im_copy(p, k, j).wait_recv()
+            shared.append(sib_image(p, k, 2))
+            shared[-1].start()
+    dest = sibling(META.at[core], 2, 0)
+    dest.start()
+
+    row = lax.broadcasted_iota(jnp.int32, (8, 1), 0)
+    expert = 4 * (4 * z + x) + lax.rem(row + 2 * core, 4)
+    expert = jnp.where(row < 4, expert, -1).astype(jnp.float32)
+    for b in range(16):
+        ids = META[core, b // 4, b % 4, pl.ds(0, 8), :]
+        weights = META[core, b // 4, b % 4, pl.ds(8, 8), :]
+        total = jnp.zeros((8, 128), jnp.float32)
+        for i in range(8):
+            total += jnp.where(ids[i:i + 1] == expert, weights[i:i + 1], 0.0)
+        GB[pl.ds(8 * b, 8), :] = total
+    gates[...] = jnp.transpose(GB[...])
+
+    for c in shared:
+        c.wait_recv()
+    dest.wait_recv()
+    lane = lax.broadcasted_iota(jnp.int32, (1, 128), 1)
+    token = lax.broadcasted_iota(jnp.int32, (128, 128), 0) + 128 * ((z * 4 + x) * 2 + core)
+    token = token.astype(jnp.float32)
+
+    def group(g, carry):
+        placed, present = carry
+        c, gz = g // 4, lax.rem(g, 4)
+        spots = [META[c, gz, i, pl.ds(16, 8), :][:1] for i in range(4)]
+        hot = [
+            (jnp.where(lane < 64, spots[i], spots[i + 1]) == token).astype(jnp.float32)
+            for i in (0, 2)
+        ]
+        present += jnp.sum(hot[0] + hot[1], axis=1, keepdims=True)
+        hot = jnp.concatenate(hot, axis=1).astype(jnp.bfloat16)
+        placed += jnp.dot(
+            hot, IMG[c, gz].reshape(256, QUARTER), preferred_element_type=jnp.float32
+        )
+        return placed, present
+
+    placed, present = lax.fori_loop(
+        0, 8, group, (jnp.zeros((128, QUARTER), jnp.float32), jnp.zeros((128, 1), jnp.float32))
+    )
+    whole = jnp.where(present > 0.5, placed, text[...].astype(jnp.float32))
+    merged[...] = whole.astype(jnp.bfloat16)
+    squares = jnp.sum(whole * whole, axis=1, keepdims=True)
+    SQ[y] = jnp.broadcast_to(squares, (128, 128))
+    sq = [
+        pltpu.make_async_remote_copy(
+            src_ref=SQ.at[y], dst_ref=SQ.at[y], send_sem=sq_send.at[d - 1], recv_sem=sq_recv.at[d - 1],
+            device_id=device(moved(me, "y", d), core), device_id_type=MESH,
+        )
+        for d in (1, 2, 3)
+    ]
+    for c in sq:
+        c.start()
+    for c in sq:
+        c.wait()
+    mean = (SQ[0] + SQ[1] + SQ[2] + SQ[3])[:, :1] / 4096.0
+    scale = lax.rsqrt(mean + 1e-06)
+    normed[...] = (whole * scale * gain[pl.ds(y, 1), :]).astype(jnp.bfloat16)
+    for k in range(2):
+        for j in range(3):
+            me_copy(k, j).wait_send()
+        for p in range(2):
+            for j in range(4):
+                im_copy(p, k, j).wait_send()
+    for c in shared:
+        c.wait_send()
+    dest.wait_send()
+
+
+def merge(text, image, meta, gain):
+    bf, f32 = jnp.bfloat16, jnp.float32
+    vmem = pl.BlockSpec(memory_space=pltpu.VMEM)
+    dma = pltpu.SemaphoreType.DMA
+    return pl.pallas_call(
+        image_kernel,
+        out_shape=[
+            jax.ShapeDtypeStruct(text.shape, bf),
+            jax.ShapeDtypeStruct(text.shape, bf),
+            jax.ShapeDtypeStruct((128, 128), f32),
+        ],
+        in_specs=[vmem] * 4,
+        out_specs=[vmem] * 3,
+        scratch_shapes=[
+            pltpu.VMEM((2, 4, 4, 64, QUARTER), bf),
+            pltpu.VMEM((2, 4, 4, 24, 128), f32),
+            pltpu.VMEM((4, 128, 128), f32),
+            pltpu.VMEM((128, 128), f32),
+            dma((2, 2, 4)),
+            dma((2, 2, 4)),
+            dma((2, 3)),
+            dma((2, 3)),
+            dma((3, 7)),
+            dma((3, 7)),
+            dma((3,)),
+            dma((3,)),
+        ],
+        cost_estimate=pl.CostEstimate(flops=1 << 29, bytes_accessed=6 << 20, transcendentals=128),
+        compiler_params=pltpu.CompilerParams(
+            collective_id=1, has_side_effects=True, vmem_limit_bytes=40 << 20
+        ),
+    )(text, image, meta, gain)
+
+
 def on_device(
     text_rows, image_rows, image_dest, norm_gain, expert_ids, gate_weights, w_gate, w_up, w_down
 ):
-    seq_count = lax.axis_size("seq")
-    tok_dev = text_rows.shape[0]
-    s = lax.axis_index("seq")
-    y = lax.axis_index("exp")
-    rows_all = lax.all_gather(image_rows, "seq").reshape(-1, QUARTER)
-    dest_all = lax.all_gather(image_dest, "seq").reshape(1, -1)
-    place_hot = (jnp.arange(tok_dev, dtype=jnp.int32) + s * tok_dev)[:, None] == dest_all
-    placed = jnp.dot(place_hot.astype(jnp.bfloat16), rows_all, preferred_element_type=jnp.float32)
-    present = jnp.any(place_hot, axis=1)
-    merged = jnp.where(present[:, None], placed.astype(jnp.bfloat16), text_rows)
-    merged_f = merged.astype(jnp.float32)
-    squares = lax.psum(jnp.sum(merged_f * merged_f, axis=1, keepdims=True), "exp")
-    scale = lax.rsqrt(squares / 4096 + 1e-06)
-    gain = lax.dynamic_slice(norm_gain, (y * QUARTER,), (QUARTER,))
-    normed = (merged_f * scale * gain).astype(jnp.bfloat16)
-    ids = lax.all_gather(expert_ids, "seq").reshape(16, 2, tok_dev, 8)
-    weights = lax.all_gather(gate_weights, "seq").reshape(16, 2, tok_dev, 8)
-    core = s % 2
-    ids = lax.dynamic_index_in_dim(ids, core, 1, keepdims=False)
-    weights = lax.dynamic_index_in_dim(weights, core, 1, keepdims=False)
-    lane = jnp.arange(128, dtype=jnp.int32)
-    chip = s - core
-    expert = jnp.where(lane < 4, 2 * chip + (lane + 2 * core) % 4, -1)
-    gates = jnp.sum(
-        jnp.where(ids[..., None] == expert, weights[..., None], 0.0), axis=2
+    f32 = jnp.float32
+    spots = image_dest.astype(f32)
+    meta = jnp.concatenate(
+        [
+            expert_ids.astype(f32).T,
+            gate_weights.T,
+            jnp.broadcast_to(jnp.concatenate([spots, spots])[None], (8, 128)),
+        ],
+        axis=0,
     )
-    gates = gates.reshape(16, CHUNKS, ROWS, 128).transpose(1, 0, 2, 3).reshape(CHUNKS, 512, 128)
+    merged, normed, gates = merge(text_rows, image_rows, meta, norm_gain.reshape(4, QUARTER))
     return experts(normed, merged, gates, w_gate, w_up, w_down)
 
 

time: 314 us -> 240 us (0.76)
  blocking collectives: 75.5 us -> 0 us
  Pallas kernels: 208 us -> 230 us
  between operations: 14.1 us -> 0.03 us
  other arithmetic: 6.84 us -> 2.11 us
    all_gather x2 -> x0, blocking collectives: 50 us -> none  [the longest x1 26 us: on_device(): weights = lax.all_gather(gate_weights, 'seq').reshape(16, 2, tok_dev, 8)]
    pallas_call x0 -> x1, Pallas kernels: none -> 36.5 us  [merge(): pl.pallas_call(image_kernel, out_shape=[jax.ShapeDtypeStruct(text.shape,...]
    unnamed x1 -> x0, blocking collectives: 14.6 us -> none
    pallas_call x1, Pallas kernels: 208 us -> 194 us  [experts(): pl.pallas_call(expert_kernel, out_shape=[jax.ShapeDtypeStruct(merged.shap...]
    psum x1 -> x0, blocking collectives: 10.9 us -> none  [on_device(): lax.psum(jnp.sum(merged_f * merged_f, axis=1, keepdims=True), 'exp')]
    reduce_sum x1 -> x0, other arithmetic: 5.69 us -> none  [on_device(): jnp.sum(jnp.where(ids[..., None] == expert, weights[..., None], 0.0), axi...]
  transfers between devices with their start and end apart: 1 -> 0, of which waited for: 0 -> 0; matrix products, arithmetic and copies ran while one was open for 3% -> 0% of each run, Pallas kernels for 0% -> 0%
where the time goes in v2:
time: 240 us; the launch traced here: 239 us
  Pallas kernels  230 us (96%)
  local copies, waits for them, and re-layouts  6.27 us (3%)
    pallas_call x1, Pallas kernels, experts(): pl.pallas_call(expert_kernel, out_shape=[jax.ShapeDtypeStruct(merged.shap...  194 us
    pallas_call x1, Pallas kernels, merge(): pl.pallas_call(image_kernel, out_shape=[jax.ShapeDtypeStruct(text.shape,...  36.5 us
    unnamed x11, local copies, waits for them, and re-layouts  5.54 us

profile of v2, /device:TPU:0, one launch (start us, length us, event | category | flops | bytes accessed | tf_op | source)
XLA Modules:
  0.0 238.8 jit_solution(14226027683154375728)
XLA Ops:
  0.0 0.7 convert_element_type.7
  0.7 0.1 pad_maximum_fusion.1
  0.7 0.7 convert_bitcast_fusion
  1.4 0.7 pad_maximum_fusion.meta
  2.1 0.7 reshape.4.gain
  2.8 0.0 copy-start
  2.8 0.9 copy-done
  3.8 0.0 copy-start.1
  3.8 0.9 copy-done.1
  4.7 36.5 %shard_map.91 = (bf16[128,1024]{1,0:T(8,128)(2,1)S(1)}, bf16[128,1024]{1,0:T(8,128)(2,1)S(1)}, f32[128,128]{1,0:T(8,128)S(1)}) custom-call(bf16[128,1024]{1,0:T(8,128)(2,1)S(1)} %copy-done, bf16[64,1024]{1,0:T(8,128)(2,1)S(1)} %copy-done.1, f32[24,128]{1,0:T(8,128)S(1)} %pad_maximum_fusion.meta, f32[4,1024]{1,0:T(4,128)S(1)} %reshape.4.gain), custom_call_target="tpu_custom_call" | custom-call | flops 536870912 | bytes 6291456 | tf_op jit(solution)/shard_map/pallas_call | solution.py:539
  41.2 0.0 copy-start.2
  41.2 0.7 copy-done.2
  41.9 0.0 copy-start.3
  41.9 0.7 copy-done.3
  42.6 0.0 copy-start.4
  42.6 0.6 copy-done.4
  43.2 193.9 %shard_map.92 = (bf16[128,1024]{1,0:T(8,128)(2,1)}, bf16[2,4096,384]{2,1,0:T(8,128)(2,1)}, bf16[2,4096,384]{2,1,0:T(8,128)(2,1)}, bf16[2,384,4096]{2,1,0:T(8,128)(2,1)}) custom-call(bf16[128,1024]{1,0:T(8,128)(2,1)} %copy-done.3, bf16[128,1024]{1,0:T(8,128)(2,1)} %copy-done.2, f32[128,128]{1,0:T(8,128)} %copy-done.4, bf16[2,4096,384]{2,1,0:T(8,128)(2,1)} %w_gate.1, ...), custom_call_target="tpu_custom_call" | custom-call | flops 77309411328 | bytes 157286400 | tf_op jit(solution)/shard_map/pallas_call | solution.py:345
  237.2 1.7 copy.11
  (1 shorter events, 0.0 us)
Async XLA Ops:
  2.8 0.9 copy-start
  3.8 0.9 copy-start.1
  41.2 0.7 copy-start.2
  41.9 0.7 copy-start.3
  42.6 0.6 copy-start.4

commit v3 on v2

--- a/solution.py
+++ b/solution.py
@@ -41,12 +41,12 @@
 def expert_kernel(
     normed, merged, gates, w_gate, w_up, w_down,
     out, far_gate, far_up, far_down,
-    X, H, WB, WD, half1, half2, half3, full1, full2, full3,
+    X, H, WB, WD, half1, full1, full2, full3,
     own_sem, wb_sem, wd_sem, far_send, far_recv, ag_send, ag_recv, rs_send, rs_recv,
 ):
     me, core = place()
     barrier = pltpu.get_barrier_semaphore()
-    neighbours = [device(moved(me, a, d), core) for a in "xyz" for d in (1, -1)]
+    neighbours = [device(moved(me, a, d), core) for a in "xyz" for d in (1, 2, 3)]
     neighbours.append(device(me, 1 - core))
     for who in neighbours:
         pl.semaphore_signal(barrier, inc=1, device_id=who, device_id_type=MESH)
@@ -81,61 +81,61 @@
     def ag_copy(q, p, k, j):
         order = ORDERS[p]
         axis, full = order[k], order[:k]
-        way = 1 if j % 2 == 0 else -1
         cols = columns(q, p)
-        if j < 2:
+        by = (1, -1, 2)[j] if k < 2 else (1, -1, 1, -1)[j]
+        if j < 2 or k < 2:
             index = slab(q, full, me, cols)
             src = normed.at[pl.ds(ROWS * q, ROWS), cols] if k == 0 else X.at[index]
         else:
             rows = pl.ds(0, 16) if j == 2 else pl.ds(16, 16)
-            index = slab(q, full, moved(me, axis, -way), cols, rows)
+            index = slab(q, full, moved(me, axis, -by), cols, rows)
             src = X.at[index]
         return pltpu.make_async_remote_copy(
             src_ref=src, dst_ref=X.at[index],
             send_sem=ag_send.at[q, p, k, j], recv_sem=ag_recv.at[q, p, k, j],
-            device_id=device(moved(me, axis, way), core), device_id_type=MESH,
+            device_id=device(moved(me, axis, by), core), device_id_type=MESH,
         )
 
     def ag_first(q, k):
         for p in range(3):
             if k:
-                for j in (2, 3):
+                for j in range(3):
                     ag_copy(q, p, k - 1, j).wait_recv()
+            for j in range(3 if k < 2 else 2):
+                ag_copy(q, p, k, j).start()
+
+    def ag_second(q):
+        for p in range(3):
             for j in (0, 1):
-                ag_copy(q, p, k, j).start()
-
-    def ag_second(q, k):
-        for p in range(3):
-            for j in (0, 1):
-                ag_copy(q, p, k, j).wait_recv()
-                ag_copy(q, p, k, j + 2).start()
+                ag_copy(q, p, 2, j).wait_recv()
+                ag_copy(q, p, 2, j + 2).start()
 
     def ag_end(q):
         for p in range(3):
             for j in (2, 3):
                 ag_copy(q, p, 2, j).wait_recv()
             for k in range(3):
-                for j in range(4):
+                for j in range(3 if k < 2 else 4):
                     ag_copy(q, p, k, j).wait_send()
 
-    halves, fulls = (half1, half2, half3), (full1, full2, full3)
+    fulls = (full1, full2, full3)
 
     def rs_refs(q, p, k, j):
         order = ORDERS[p][::-1]
         axis, full = order[k], order[k + 1:]
         cols = columns(q, p)
-        way = 1 if j % 2 == 0 else -1
         mid = (slice(None),) * len(full)
-        if j < 2:
-            rows = pl.ds(0, 16) if j == 0 else pl.ds(16, 16)
+        by = (1, -1, 1, -1)[j] if k == 0 else (2, 1, -1)[j]
+        if k == 0 and j < 2:
+            rows = pl.ds(16 * j, 16)
             sent = slab(q, full, moved(me, axis, 2), cols, rows)
-            kept = slab(q, full, moved(me, axis, way), cols, rows)
-            got = halves[k].at[(q, j, *mid, slice(None), cols)]
+            kept = slab(q, full, moved(me, axis, by), cols, rows)
+            got = half1.at[(q, j, *mid, slice(None), cols)]
         else:
-            sent = slab(q, full, moved(me, axis, way), cols)
+            sent = slab(q, full, moved(me, axis, by), cols)
             kept = slab(q, full, me, cols)
-            got = fulls[k].at[(q, j - 2, *mid, slice(None), cols)]
-        return sent, kept, got, device(moved(me, axis, way), core)
+            got = fulls[k].at[(q, j - 2 if k == 0 else j, *mid, slice(None), cols)]
+        return sent, kept, got, device(moved(me, axis, by), core)
 
     def rs_copy(q, p, k, j):
         sent, _, got, who = rs_refs(q, p, k, j)
@@ -145,32 +145,34 @@
             device_id=who, device_id_type=MESH,
         )
 
-    def rs_first(q, k):
-        for p in range(3):
-            for j in (0, 1):
-                rs_copy(q, p, k, j).start()
-
     def f32(v):
         return v.astype(jnp.float32)
 
-    def rs_second(q, k):
+    def rs_first(q):
         for p in range(3):
             for j in (0, 1):
+                rs_copy(q, p, 0, j).start()
+
+    def rs_second(q):
+        for p in range(3):
+            for j in (0, 1):
+                rs_copy(q, p, 0, j).wait_recv()
+                _, kept, got, _ = rs_refs(q, p, 0, j)
+                X[kept] = (f32(X[kept]) + f32(got[...])).astype(jnp.bfloat16)
+                rs_copy(q, p, 0, j + 2).start()
+
+    def rs_end(q, k):
+        for p in range(3):
+            last = (2, 3) if k == 0 else (0, 1, 2)
+            kept = rs_refs(q, p, k, 2)[1]
+            total = f32(X[kept])
+            for j in last:
                 rs_copy(q, p, k, j).wait_recv()
-                _, kept, got, _ = rs_refs(q, p, k, j)
-                X[kept] = (f32(X[kept]) + f32(got[...])).astype(jnp.bfloat16)
-                rs_copy(q, p, k, j + 2).start()
-
-    def rs_end(q, k):
-        for p in range(3):
-            _, kept, a, _ = rs_refs(q, p, k, 2)
-            b = rs_refs(q, p, k, 3)[2]
-            for j in (2, 3):
-                rs_copy(q, p, k, j).wait_recv()
-            total = f32(X[kept]) + f32(a[...]) + f32(b[...])
+            for j in last:
+                total += f32(rs_refs(q, p, k, j)[2][...])
             if k < 2:
                 X[kept] = total.astype(jnp.bfloat16)
-                for j in (0, 1):
+                for j in range(3):
                     rs_copy(q, p, k + 1, j).start()
             else:
                 rows, cols = pl.ds(ROWS * q, ROWS), columns(q, p)
@@ -201,27 +203,26 @@
         ]
 
     plan = {
-        (0, 0): [lambda: ag_second(1, 2), lambda: ag_first(2, 2)],
-        (0, 3): [lambda: ag_second(2, 2), lambda: ag_first(3, 2)],
-        (0, 11): [lambda: ag_end(1)],
-        (1, 0): [lambda: ag_second(3, 2)],
-        (1, 11): [lambda: ag_end(2)],
-        (2, 11): [lambda: ag_end(3)],
+        (0, 0): [lambda: ag_first(2, 1)],
+        (0, 1): [lambda: ag_second(1), lambda: ag_first(2, 2)],
+        (0, 2): [lambda: ag_first(3, 1)],
+        (0, 4): [lambda: ag_end(1)],
+        (0, 5): [lambda: ag_second(2), lambda: ag_first(3, 2)],
+        (1, 1): [lambda: ag_second(3)],
+        (1, 8): [lambda: ag_end(2)],
+        (2, 8): [lambda: ag_end(3)],
     }
 
     def add(q, u, f, *args):
         plan.setdefault((q, u), []).append(lambda: f(*args))
 
     for q in range(CHUNKS):
-        add(q, 11, rs_first, q, 0)
+        add(q, 11, rs_first, q)
         if q < CHUNKS - 1:
-            add(q + 1, 1, rs_second, q, 0)
-            add(q + 1, 3, rs_end, q, 0)
-            add(q + 1, 6, rs_second, q, 1)
-            add(q + 1, 9, rs_end, q, 1)
-            add(q + 1, 11, rs_second, q, 2)
-            if q < CHUNKS - 2:
-                add(q + 2, 0, rs_end, q, 2)
+            add(q + 1, 1, rs_second, q)
+            add(q + 1, 4, rs_end, q, 0)
+            add(q + 1, 7, rs_end, q, 1)
+            add(q + 1, 10, rs_end, q, 2)
 
     def hooks(q, u, units):
         for (pq, pu), actions in sorted(plan.items()):
@@ -233,27 +234,21 @@
 
     for c in own:
         c.start()
-    for q in range(CHUNKS):
-        ag_first(q, 0)
-    for c in far[:2]:
-        c.start()
+    ag_first(0, 0)
+    ag_first(1, 0)
     wb_start(0, 0)
     for c in own:
         c.wait()
-    ag_second(0, 0)
     ag_first(0, 1)
-    for q in range(1, CHUNKS):
-        ag_second(q, 0)
-    for c in far[2:4]:
+    ag_first(1, 1)
+    ag_first(0, 2)
+    for c in far[:2]:
         c.start()
-    ag_second(0, 1)
-    ag_first(0, 2)
-    for q in range(1, CHUNKS):
-        ag_first(q, 1)
-    far[4].start()
-    for q in range(1, CHUNKS):
-        ag_second(q, 1)
-    ag_second(0, 2)
+    for q in range(2, CHUNKS):
+        ag_first(q, 0)
+    for c in far[2:]:
+        c.start()
+    ag_second(0)
     ag_first(1, 2)
     ag_end(0)
 
@@ -323,16 +318,15 @@
 
     lax.fori_loop(0, CHUNKS, chunk, 0)
     last = CHUNKS - 1
-    rs_end(last - 1, 2)
+    rs_second(last)
     for k in range(3):
-        rs_second(last, k)
         rs_end(last, k)
     for c in far:
         c.wait_send()
     for q in range(CHUNKS):
         for p in range(3):
             for k in range(3):
-                for j in range(4):
+                for j in range(4 if k == 0 else 3):
                     rs_copy(q, p, k, j).wait_send()
 
 
@@ -358,11 +352,9 @@
             pltpu.VMEM((2, 4096, 768), bf),
             pltpu.VMEM((2, 4, 384, TILE), bf),
             pltpu.VMEM((CHUNKS, 2, 4, 4, 16, QUARTER), bf),
-            pltpu.VMEM((CHUNKS, 2, 4, 16, QUARTER), bf),
-            pltpu.VMEM((CHUNKS, 2, 16, QUARTER), bf),
             pltpu.VMEM((CHUNKS, 2, 4, 4, ROWS, QUARTER), bf),
-            pltpu.VMEM((CHUNKS, 2, 4, ROWS, QUARTER), bf),
-            pltpu.VMEM((CHUNKS, 2, ROWS, QUARTER), bf),
+            pltpu.VMEM((CHUNKS, 3, 4, ROWS, QUARTER), bf),
+            pltpu.VMEM((CHUNKS, 3, ROWS, QUARTER), bf),
             dma((CHUNKS,)),
             dma((2, 2)),
             dma((2, 2)),

time: 240 us -> 233 us (0.971)
  Pallas kernels: 230 us -> 223 us
    pallas_call x1, Pallas kernels: 194 us -> 187 us  [experts(): pl.pallas_call(expert_kernel, out_shape=[jax.ShapeDtypeStruct(merged.shap...]
where the time goes in v3:
time: 233 us; the launch traced here: 232 us
  Pallas kernels  223 us (96%)
  local copies, waits for them, and re-layouts  6.27 us (3%)
    pallas_call x1, Pallas kernels, experts(): pl.pallas_call(expert_kernel, out_shape=[jax.ShapeDtypeStruct(merged.shap...  187 us
    pallas_call x1, Pallas kernels, merge(): pl.pallas_call(image_kernel, out_shape=[jax.ShapeDtypeStruct(text.shape,...  36.5 us
    unnamed x11, local copies, waits for them, and re-layouts  5.54 us

profile of v3, /device:TPU:0, one launch (start us, length us, event | category | flops | bytes accessed | tf_op | source)
XLA Modules:
  0.0 231.6 jit_solution(13533374988993396815)
XLA Ops:
  0.0 0.7 convert_element_type.7
  0.7 0.1 pad_maximum_fusion.1
  0.7 0.7 convert_bitcast_fusion
  1.4 0.7 pad_maximum_fusion.meta
  2.1 0.7 reshape.4.gain
  2.8 0.0 copy-start
  2.8 0.9 copy-done
  3.8 0.0 copy-start.1
  3.8 0.9 copy-done.1
  4.7 36.5 %shard_map.91 = (bf16[128,1024]{1,0:T(8,128)(2,1)S(1)}, bf16[128,1024]{1,0:T(8,128)(2,1)S(1)}, f32[128,128]{1,0:T(8,128)S(1)}) custom-call(bf16[128,1024]{1,0:T(8,128)(2,1)S(1)} %copy-done, bf16[64,1024]{1,0:T(8,128)(2,1)S(1)} %copy-done.1, f32[24,128]{1,0:T(8,128)S(1)} %pad_maximum_fusion.meta, f32[4,1024]{1,0:T(4,128)S(1)} %reshape.4.gain), custom_call_target="tpu_custom_call" | custom-call | flops 536870912 | bytes 6291456 | tf_op jit(solution)/shard_map/pallas_call | solution.py:531
  41.2 0.0 copy-start.2
  41.2 0.7 copy-done.2
  41.9 0.0 copy-start.3
  41.9 0.7 copy-done.3
  42.6 0.0 copy-start.4
  42.6 0.6 copy-done.4
  43.2 186.7 %shard_map.92 = (bf16[128,1024]{1,0:T(8,128)(2,1)}, bf16[2,4096,384]{2,1,0:T(8,128)(2,1)}, bf16[2,4096,384]{2,1,0:T(8,128)(2,1)}, bf16[2,384,4096]{2,1,0:T(8,128)(2,1)}) custom-call(bf16[128,1024]{1,0:T(8,128)(2,1)} %copy-done.3, bf16[128,1024]{1,0:T(8,128)(2,1)} %copy-done.2, f32[128,128]{1,0:T(8,128)} %copy-done.4, bf16[2,4096,384]{2,1,0:T(8,128)(2,1)} %w_gate.1, ...), custom_call_target="tpu_custom_call" | custom-call | flops 77309411328 | bytes 157286400 | tf_op jit(solution)/shard_map/pallas_call | solution.py:339
  230.0 1.7 copy.11
  (1 shorter events, 0.0 us)
Async XLA Ops:
  2.8 0.9 copy-start
  3.8 0.9 copy-start.1
  41.2 0.7 copy-start.2
  41.9 0.7 copy-start.3
  42.6 0.6 copy-start.4

commit v4 on v3

--- a/solution.py
+++ b/solution.py
@@ -385,7 +385,7 @@
 ):
     me, core = place()
     barrier = pltpu.get_barrier_semaphore()
-    neighbours = [device(moved(me, a, d), core) for a in "zx" for d in (1, -1)]
+    neighbours = [device(moved(me, a, d), core) for a in "zx" for d in (1, 2, 3)]
     neighbours += [device(moved(me, "y", d), core) for d in (1, 2, 3)]
     neighbours.append(device(me, 1 - core))
     for who in neighbours:
@@ -400,9 +400,10 @@
 
     def im_copy(p, k, j):
         axis, full = IMAGES[p][k], IMAGES[p][:k]
-        way = 1 if j % 2 == 0 else -1
-        at = me if j < 2 else moved(me, axis, -way)
-        rows = pl.ds(0, 64) if j < 2 else pl.ds(32 * (j - 2), 32)
+        way = (1, -1, 2)[j] if k == 0 else (1, -1, 1, -1)[j]
+        whole = k == 0 or j < 2
+        at = me if whole else moved(me, axis, -way)
+        rows = pl.ds(0, 64) if whole else pl.ds(32 * (j - 2), 32)
         part = IMG.at[(*spot(full, at), rows, pl.ds(512 * p, 512))]
         return pltpu.make_async_remote_copy(
             src_ref=part, dst_ref=part, send_sem=im_send.at[p, k, j], recv_sem=im_recv.at[p, k, j],
@@ -411,8 +412,8 @@
 
     def me_copy(k, j):
         axis, full = IMAGES[0][k], IMAGES[0][:k]
-        way = 1 if j % 2 == 0 else -1
-        part = META.at[spot(full, me if j < 2 else moved(me, axis, -1))]
+        way = (1, -1, 2)[j]
+        part = META.at[spot(full, me)]
         return pltpu.make_async_remote_copy(
             src_ref=part, dst_ref=part, send_sem=me_send.at[k, j], recv_sem=me_recv.at[k, j],
             device_id=device(moved(me, axis, way), core), device_id_type=MESH,
@@ -436,22 +437,22 @@
     for c in shared:
         c.start()
     for k in range(2):
-        for j in (0, 1):
+        for j in range(3):
             me_copy(k, j).start()
-            for p in range(2):
-                im_copy(p, k, j).start()
-        me_copy(k, 0).wait_recv()
-        me_copy(k, 2).start()
+            if j < 2 or k == 0:
+                for p in range(2):
+                    im_copy(p, k, j).start()
         for j in (0, 1):
             for p in range(2):
                 im_copy(p, k, j).wait_recv()
-                im_copy(p, k, j + 2).start()
+                if k:
+                    im_copy(p, k, j + 2).start()
                 shared.append(sib_image(p, k, 3 if j == 0 else 1))
                 shared[-1].start()
-        me_copy(k, 1).wait_recv()
-        me_copy(k, 2).wait_recv()
+        for j in range(3):
+            me_copy(k, j).wait_recv()
         for p in range(2):
-            for j in (2, 3):
+            for j in (2, 3) if k else (2,):
                 im_copy(p, k, j).wait_recv()
             shared.append(sib_image(p, k, 2))
             shared[-1].start()
@@ -517,7 +518,7 @@
         for j in range(3):
             me_copy(k, j).wait_send()
         for p in range(2):
-            for j in range(4):
+            for j in range(4 if k else 3):
                 im_copy(p, k, j).wait_send()
     for c in shared:
         c.wait_send()

time: 233 us -> 233 us (level)
  no operation moved by 1% of the time
where the time goes in v4:
time: 233 us; the launch traced here: 232 us
  Pallas kernels  223 us (96%)
  local copies, waits for them, and re-layouts  6.27 us (3%)
    pallas_call x1, Pallas kernels, experts(): pl.pallas_call(expert_kernel, out_shape=[jax.ShapeDtypeStruct(merged.shap...  188 us
    pallas_call x1, Pallas kernels, merge(): pl.pallas_call(image_kernel, out_shape=[jax.ShapeDtypeStruct(text.shape,...  35.5 us
    unnamed x11, local copies, waits for them, and re-layouts  5.54 us

profile of v4, /device:TPU:0, one launch (start us, length us, event | category | flops | bytes accessed | tf_op | source)
XLA Modules:
  0.0 231.7 jit_solution(17937117275192729779)
XLA Ops:
  0.0 0.7 convert_element_type.7
  0.7 0.1 pad_maximum_fusion.1
  0.7 0.7 convert_bitcast_fusion
  1.4 0.7 pad_maximum_fusion.meta
  2.1 0.7 reshape.4.gain
  2.8 0.0 copy-start
  2.8 0.9 copy-done
  3.8 0.0 copy-start.1
  3.8 0.9 copy-done.1
  4.7 35.5 %shard_map.91 = (bf16[128,1024]{1,0:T(8,128)(2,1)S(1)}, bf16[128,1024]{1,0:T(8,128)(2,1)S(1)}, f32[128,128]{1,0:T(8,128)S(1)}) custom-call(bf16[128,1024]{1,0:T(8,128)(2,1)S(1)} %copy-done, bf16[64,1024]{1,0:T(8,128)(2,1)S(1)} %copy-done.1, f32[24,128]{1,0:T(8,128)S(1)} %pad_maximum_fusion.meta, f32[4,1024]{1,0:T(4,128)S(1)} %reshape.4.gain), custom_call_target="tpu_custom_call" | custom-call | flops 536870912 | bytes 6291456 | tf_op jit(solution)/shard_map/pallas_call | solution.py:532
  40.2 0.0 copy-start.2
  40.2 0.7 copy-done.2
  40.9 0.0 copy-start.3
  40.9 0.7 copy-done.3
  41.6 0.0 copy-start.4
  41.6 0.6 copy-done.4
  42.3 187.8 %shard_map.92 = (bf16[128,1024]{1,0:T(8,128)(2,1)}, bf16[2,4096,384]{2,1,0:T(8,128)(2,1)}, bf16[2,4096,384]{2,1,0:T(8,128)(2,1)}, bf16[2,384,4096]{2,1,0:T(8,128)(2,1)}) custom-call(bf16[128,1024]{1,0:T(8,128)(2,1)} %copy-done.3, bf16[128,1024]{1,0:T(8,128)(2,1)} %copy-done.2, f32[128,128]{1,0:T(8,128)} %copy-done.4, bf16[2,4096,384]{2,1,0:T(8,128)(2,1)} %w_gate.1, ...), custom_call_target="tpu_custom_call" | custom-call | flops 77309411328 | bytes 157286400 | tf_op jit(solution)/shard_map/pallas_call | solution.py:339
  230.1 1.7 copy.11
  (1 shorter events, 0.0 us)
Async XLA Ops:
  2.8 0.9 copy-start
  3.8 0.9 copy-start.1
  40.2 0.7 copy-start.2
  40.9 0.7 copy-start.3
  41.6 0.6 copy-start.4
